TPU v7x, 32 devices: a whole 2x2x4 slice. The times are simulated.
32 devices in a mesh: tm: 8 (over z, y), height: 4 (over x, core).
Axes of the slice: x: 2, y: 2, z: 4, core: 2. Of those that a mesh axis runs over, the one named last changes fastest.
Arguments:
- latents: bfloat16 [16, 16, 128, 256], P('tm', 'height'), may hold values from -6 to 6
- conv_first: bfloat16 [3, 3, 3, 256, 256], replicated, may hold values from -0.078125 to 0.078125
- conv_second: bfloat16 [3, 3, 3, 256, 256], replicated, may hold values from -0.078125 to 0.078125
- codebook: bfloat16 [262144, 256], P('height'), may hold values from -13 to 13
- codes: int32 [16, 16, 128], P('tm', 'height'), may hold values from 0 to 262143, as said below
- upstream: bfloat16 [16, 16, 128, 256], P('tm', 'height'), may hold values from -6 to 6
Outputs:
- grad_latent: bfloat16 [16, 16, 128, 256], P('tm', 'height')
- codebook_grad: bfloat16 [262144, 256], P(('height', 'tm'))
Inputs may be any that keep to these rules, and one draw needn't show every extreme that they name: Each device's 1024 cells hold at most 64 codes of any one aligned range of 8192 codes; some ranges receive exactly 64 from every device.
All inputs are finite; a program needn't handle non-finite values.
Results may differ from a plain program's by a relative error of at most 0.0085.
Values may be sent and summed in bfloat16 or wider, within the bound.
No kernel may reach another device: no remote copies, remote signals or barrier semaphores. Data moves between devices by JAX's collectives and lax.ppermute only.
A program may use at most 128 MiB of HBM per device.

v0:
```python
import jax
import jax.numpy as jnp
from jax import lax
from jax.sharding import PartitionSpec as P

COMMIT = 0.25


def passed_along(x, axis, by):
    count = lax.axis_size(axis)
    pairs = [(i, i + by) for i in range(count) if 0 <= i + by < count]
    return lax.ppermute(x, axis, pairs)


def extended_2(block, sides, width):
    for axis, dim in sides:
        count = lax.axis_size(axis)
        forward = [(i, i + 1) for i in range(count - 1)]
        backward = [(target, source) for source, target in forward]
        low = lax.ppermute(
            lax.slice_in_dim(block, block.shape[dim] - width, None, axis=dim), axis, forward
        )
        high = lax.ppermute(lax.slice_in_dim(block, 0, width, axis=dim), axis, backward)
        block = jnp.concatenate([low, block, high], axis=dim)
    return block


def norm_act(video):
    values = video.astype(jnp.float32)
    scaled = values * lax.rsqrt(jnp.mean(values * values, -1, keepdims=True) + 1e-06)
    return jax.nn.silu(scaled).astype(jnp.bfloat16)


def conv_block(video, weight):
    frames, rows, columns, channels = video.shape
    active = norm_act(video)
    earlier = passed_along(active, "tm", 1)
    extended = jnp.concatenate([earlier, active], 0)
    extended = extended_2(extended, (("height", 1),), 1)
    extended = jnp.pad(extended, ((0, 0), (0, 0), (1, 1), (0, 0)))
    pieces = [
        extended[step_t : step_t + frames, step_h : step_h + rows, step_w : step_w + columns, :]
        for step_t in range(3)
        for step_h in range(3)
        for step_w in range(3)
    ]
    patch = jnp.concatenate(pieces, -1).reshape(frames * rows * columns, 27 * channels)
    conv = jnp.dot(
        patch, weight.reshape(27 * channels, channels), preferred_element_type=jnp.float32
    )
    return (video.astype(jnp.float32) + conv.reshape(video.shape)).astype(jnp.bfloat16)


def rotate_back(latent, quant, upward):
    lat_norm = jnp.sqrt(jnp.sum(latent * latent, -1, keepdims=True) + 1e-06)
    quant_norm = jnp.sqrt(jnp.sum(quant * quant, -1, keepdims=True) + 1e-06)
    lat_unit = latent / lat_norm
    quant_unit = quant / quant_norm
    cosine = jnp.sum(lat_unit * quant_unit, -1, keepdims=True)
    summed = lat_unit + quant_unit
    turned = upward - summed * (jnp.sum(summed * upward, -1, keepdims=True) / (1.0 + cosine))
    turned = turned + 2.0 * lat_unit * jnp.sum(quant_unit * upward, -1, keepdims=True)
    return quant_norm / lat_norm * turned + 2.0 * COMMIT * (latent - quant)


def on_device(latents, conv_first, conv_second, codebook, codes, upstream):
    first = conv_block(latents, conv_first)
    encoded = conv_block(first, conv_second)
    frames, rows, columns, channels = encoded.shape
    cells = frames * rows * columns
    latent_flat = encoded.reshape(cells, channels).astype(jnp.float32)
    code_flat = codes.reshape(cells)
    rows_held = codebook.shape[0]
    shard_base = lax.axis_index("height") * rows_held
    tiles = lax.axis_size("tm")
    groups = lax.axis_size("height")
    owners = tiles * groups
    range_rows = rows_held // tiles
    capacity = 2 * cells // owners
    block_id = code_flat // range_rows
    target_dev = block_id % tiles * groups + block_id // tiles
    hits = (target_dev[:, None] == jnp.arange(owners, dtype=jnp.int32)[None, :]).astype(jnp.int32)
    place_rank = jnp.sum(jnp.cumsum(hits, 0) * hits, 1) - 1
    slot_index = target_dev * capacity + place_rank
    slot_codes = jnp.full((owners * capacity,), -1, jnp.int32).at[slot_index].set(code_flat)
    owner_codes = lax.all_to_all(
        slot_codes.reshape(owners, capacity),
        ("tm", "height"),
        split_axis=0,
        concat_axis=0,
        tiled=True,
    )
    present = owner_codes >= 0
    local_rows = jnp.clip(owner_codes - shard_base, 0, rows_held - 1)
    found_rows = jnp.take(codebook, local_rows, axis=0)
    found_rows = jnp.where(present[..., None], found_rows, jnp.zeros_like(found_rows))
    rows_back = lax.all_to_all(
        found_rows, ("tm", "height"), split_axis=0, concat_axis=0, tiled=True
    )
    quant = jnp.take(rows_back.reshape(owners * capacity, channels), slot_index, axis=0).astype(
        jnp.float32
    )
    upward = upstream.reshape(cells, channels).astype(jnp.float32)
    grad_flat = rotate_back(latent_flat, quant, upward)
    diff = (quant - latent_flat).astype(jnp.bfloat16)
    term_slots = jnp.zeros((owners * capacity, channels), jnp.bfloat16).at[slot_index].set(diff)
    owner_terms = lax.all_to_all(
        term_slots.reshape(owners, capacity, channels),
        ("tm", "height"),
        split_axis=0,
        concat_axis=0,
        tiled=True,
    )
    tile_base = shard_base + lax.axis_index("tm") * range_rows
    target_rows = jnp.where(present, owner_codes - tile_base, range_rows)
    sums = (
        jnp.zeros((range_rows, channels), jnp.float32)
        .at[target_rows.reshape(-1)]
        .add(owner_terms.reshape(-1, channels).astype(jnp.float32), mode="drop")
    )
    grad_latent = grad_flat.astype(jnp.bfloat16).reshape(upstream.shape)
    return (grad_latent, (2.0 * sums).astype(jnp.bfloat16))


def solution(mesh):
    return jax.shard_map(
        on_device,
        mesh=mesh,
        in_specs=(
            P("tm", "height", None, None),
            P(),
            P(),
            P("height", None),
            P("tm", "height", None),
            P("tm", "height", None, None),
        ),
        out_specs=(P("tm", "height", None, None), P(("height", "tm"), None)),
        check_vma=False,
    )
```

profile of v0, /device:TPU:1, one launch (start us, length us, event | category | flops | bytes accessed | tf_op | source)
XLA Modules:
  0.0 240.4 jit_solution(13178134788922272500)
XLA Ops:
  0.6 1.4 fusion.27
  2.7 2.2 fusion.21
  4.8 4.8 %collective-permute-start = (bf16[2,4,128,256]{3,2,1,0:T(8,128)(2,1)}, bf16[2,4,128,256]{3,2,1,0:T(8,128)(2,1)}, u32[]{:S(2)}, u32[]{:S(2)}) collective-permute-start(bf16[2,4,128,256]{3,2,1,0:T(8,128)(2,1)} %fusion.21), channel_id=1, source_target_pairs={{0,4},{4,8},{8,12},{12,16},{16,20},{20,24},{24,28},{1,5},{5,9},{9,... | collective-permute-start | bytes 1572872 | tf_op jit(solution)/shard_map/ppermute | solution.py:12
  11.0 17.5 %reduce-window.6 = s32[32,8,128]{2,1,0:T(8,128)} reduce-window(s32[32,8,128]{2,1,0:T(8,128)} %fusion.40, s32[]{:T(128)} %constant.98.clone.1), window={size=1x1x128 pad=0_0x0_0x127_0}, to_apply=%region_0.0 | reduce-window | flops 4161536 | bytes 262148 | tf_op jit(solution)/shard_map/reduce-window
  28.4 1.7 slice.268
  36.2 4.5 %scatter_custom_fusion = s32[2048]{0:T(1024)S(1)} fusion(s32[1024]{0:T(1024)S(1)} %bitcast.81, s32[1024]{0:T(1024)} %bitcast.73, s32[]{:T(128)} %constant.101.clone.1), kind=kCustom, calls=%fused_computation.207 | custom fusion | bytes 8704 | tf_op jit(solution)/shard_map/scatter | solution.py:85
  41.4 4.8 %all-to-all-start = ((s32[32,1,64]{2,1,0:T(1,128)}), s32[32,1,64]{2,1,0:T(1,128)S(1)}, u32[]{:S(2)}, u32[]{:S(2)}) async-start(s32[32,1,64]{2,1,0:T(1,128)} %all_to_all.12), calls=%async_computation | async-start | bytes 32768 | tf_op jit(solution)/shard_map/all_to_all | solution.py:86
  48.8 1.9 pad_maximum_fusion.7
  50.7 3.5 %collective-permute-start.1 = (bf16[4,1,128,256]{3,2,1,0:T(8,128)(2,1)}, bf16[4,1,128,256]{3,2,1,0:T(8,128)(2,1)}, u32[]{:S(2)}, u32[]{:S(2)}) collective-permute-start(bf16[4,1,128,256]{3,2,1,0:T(8,128)(2,1)} %get-tuple-element.11), channel_id=1, source_target_pairs={{0,1},{1,2},{2,3},{4,5},{5,6},{6,7},{8,9},{9,10},{10,11},{12,13},{... | collective-permute-start | bytes 786440 | tf_op jit(solution)/shard_map/ppermute | solution.py:20
  54.3 1.9 collective-permute-start.2
  59.5 2.8 %collective-permute-done.2 = bf16[4,1,128,256]{3,2,1,0:T(8,128)(2,1)} collective-permute-done((bf16[4,1,128,256]{3,2,1,0:T(8,128)(2,1)}, bf16[4,1,128,256]{3,2,1,0:T(8,128)(2,1)}, u32[]{:S(2)}, u32[]{:S(2)}) %collective-permute-start.2) | collective-permute-done | bytes 262176 | tf_op jit(solution)/shard_map/ppermute | solution.py:23
  62.3 2.2 select_maximum_fusion.3
  64.5 2.1 pad_maximum_fusion
  71.0 3.9 %fusion.28 = (f32[2,4,128]{2,1,0:T(4,128)S(1)}, bf16[2,4,128,256]{3,2,1,0:T(8,128)(2,1)S(1)}) fusion(bf16[2,4,128,6912]{3,2,1,0:T(8,128)(2,1)S(1)} %slice_dynamic-update-slice_fusion.24, bf16[6912,256,1,1]{1,0,3,2:T(8,128)(2,1)S(1)} %bitcast.60, bf16[2,4,128,256]{3,2,1,0:T(8,128)(2,1)S(1)} %copy-done.6), kind=kOutput, calls=%fused_computation.58 | convolution fusion | flops 3625450496 | bytes 18747392 | tf_op jit(solution)/shard_map/dot_general | solution.py:48
  75.3 3.1 %collective-permute-start.3 = (bf16[2,4,128,256]{3,2,1,0:T(8,128)(2,1)S(1)}, bf16[2,4,128,256]{3,2,1,0:T(8,128)(2,1)S(1)}, u32[]{:S(2)}, u32[]{:S(2)}) collective-permute-start(bf16[2,4,128,256]{3,2,1,0:T(8,128)(2,1)S(1)} %fusion.17), channel_id=1, source_target_pairs={{0,4},{4,8},{8,12},{12,16},{16,20},{20,24},{24,28},{1,5},{5,9},{9,... | collective-permute-start | bytes 1572872 | tf_op jit(solution)/shard_map/ppermute | solution.py:12
  78.5 23.8 %gather_fusion = bf16[2048,256]{1,0:T(8,128)(2,1)S(1)} fusion(bf16[65536,256]{1,0:T(8,128)(2,1)} %param.9, s32[2048]{0:T(1024)S(1)} %broadcast_clamp_fusion), kind=kCustom, calls=%fused_computation | custom fusion | bytes 2105344 | tf_op jit(solution)/shard_map/jit(_take)/gather | solution.py:95
  102.3 33.0 %collective-permute-start.4 = (bf16[4,1,128,256]{3,2,1,0:T(8,128)(2,1)S(1)}, bf16[4,1,128,256]{3,2,1,0:T(8,128)(2,1)S(1)}, u32[]{:S(2)}, u32[]{:S(2)}) collective-permute-start(bf16[4,1,128,256]{3,2,1,0:T(8,128)(2,1)S(1)} %get-tuple-element.7), channel_id=1, source_target_pairs={{0,1},{1,2},{2,3},{4,5},{5,6},{6,7},{8,9},{9,10},{10,11},{12,13},{... | collective-permute-start | bytes 786440 | tf_op jit(solution)/shard_map/ppermute | solution.py:20
  135.4 1.9 collective-permute-start.5
  137.3 1.5 select_select_fusion
  138.8 14.3 %all-to-all-start.1 = ((bf16[32,64,256]{2,1,0:T(8,128)(2,1)}), bf16[32,64,256]{2,1,0:T(8,128)(2,1)S(1)}, u32[]{:S(2)}, u32[]{:S(2)}) async-start(bf16[32,64,256]{2,1,0:T(8,128)(2,1)} %select_select_fusion), calls=%async_computation.1 | async-start | bytes 2097152 | tf_op jit(solution)/shard_map/all_to_all | solution.py:97
  153.2 2.1 select_maximum_fusion
  155.3 1.6 pad_maximum_fusion.1
  160.5 4.5 %multiply_reduce_fusion.1 = (f32[2,4,128]{2,1,0:T(4,128)}, f32[2,4,128,256]{3,2,1,0:T(8,128)S(1)}) fusion(bf16[2,4,128,6912]{3,2,1,0:T(8,128)(2,1)S(1)} %slice_dynamic-update-slice_fusion, bf16[6912,256,1,1]{1,0,3,2:T(8,128)(2,1)S(1)} %bitcast.85, bf16[2,4,128,256]{3,2,1,0:T(8,128)(2,1)S(1)} %copy-done.8), kind=kOutput, calls=%fused_computation.64 | convolution fusion | flops 3625450496 | bytes 19271680 | tf_op jit(solution)/shard_map/dot_general | solution.py:48
  165.0 13.5 %all-to-all-done.1 = bf16[32,64,256]{2,1,0:T(8,128)(2,1)S(1)} async-done(((bf16[32,64,256]{2,1,0:T(8,128)(2,1)}), bf16[32,64,256]{2,1,0:T(8,128)(2,1)S(1)}, u32[]{:S(2)}, u32[]{:S(2)}) %all-to-all-start.1) | async-done | bytes 1048608 | tf_op jit(solution)/shard_map/all_to_all | solution.py:97
  178.5 3.9 %gather_fusion.1 = bf16[1024,256]{1,0:T(8,128)(2,1)S(1)} fusion(bf16[2048,256]{1,0:T(8,128)(2,1)S(1)} %bitcast.61, s32[1024]{0:T(1024)S(1)} %copy-done.15), kind=kCustom, calls=%fused_computation.1 | custom fusion | bytes 1052672 | tf_op jit(solution)/shard_map/jit(_take)/gather | solution.py:100
  183.5 6.1 %scatter_custom_fusion.1 = bf16[2048,256]{1,0:T(8,128)(2,1)} fusion(s32[1024]{0:T(1024)} %bitcast.83, bf16[1024,256]{1,0:T(8,128)(2,1)S(1)} %get-tuple-element.13, bf16[]{:T(256)} %constant.113.clone.1), kind=kCustom, calls=%fused_computation.118 | custom fusion | bytes 1049088 | tf_op jit(solution)/shard_map/scatter | solution.py:106
  189.6 4.6 %all-to-all-start.2 = ((bf16[32,64,256]{2,1,0:T(8,128)(2,1)}), bf16[32,64,256]{2,1,0:T(8,128)(2,1)}, u32[]{:S(2)}, u32[]{:S(2)}) async-start(bf16[32,64,256]{2,1,0:T(8,128)(2,1)} %bitcast.64), calls=%async_computation.2 | async-start | bytes 2097152 | tf_op jit(solution)/shard_map/all_to_all | solution.py:107
  197.0 2.3 multiply_reduce_fusion
  199.4 2.9 %fusion.26 = bf16[2,4,128,256]{3,2,1,0:T(8,128)(2,1)} fusion(f32[2,4,128,256]{3,2,1,0:T(8,128)} %copy-done.4, bf16[2,4,128,256]{3,2,1,0:T(8,128)(2,1)} %param.11, f32[2,4,128]{2,1,0:T(4,128)S(1)} %get-tuple-element.22, f32[2,4,128]{2,1,0:T(4,128)S(1)} %get-tuple-element.21, f32[2,4,128]{2,1,0:T(4,128)S(1)} %get-tuple-element.15, ...), kind=kLoop, calls=%fused_computation.56 | loop fusion | flops 3932160 | bytes 2642944 | tf_op jit(solution)/shard_map/convert_element_type | solution.py:121
  202.2 17.4 %all-to-all-done.2 = bf16[32,64,256]{2,1,0:T(8,128)(2,1)} async-done(((bf16[32,64,256]{2,1,0:T(8,128)(2,1)}), bf16[32,64,256]{2,1,0:T(8,128)(2,1)}, u32[]{:S(2)}, u32[]{:S(2)}) %all-to-all-start.2) | async-done | bytes 1048608 | tf_op jit(solution)/shard_map/all_to_all | solution.py:107
  219.6 14.6 %scatter_custom_fusion.2 = f32[8192,256]{1,0:T(8,128)} fusion(s32[2048]{0:T(1024)S(1)} %bitcast.84, f32[]{:T(128)} %constant.114.clone.1, bf16[2048,256]{1,0:T(8,128)(2,1)} %bitcast.32), kind=kCustom, calls=%fused_computation.8 | custom fusion | flops 1048576 | bytes 9437188 | tf_op jit(solution)/shard_map/scatter-add | solution.py:119
  234.3 6.1 %multiply_convert_fusion = bf16[8192,256]{1,0:T(8,128)(2,1)} fusion(f32[8192,256]{1,0:T(8,128)} %scatter_custom_fusion.2), kind=kLoop, calls=%fused_computation.5 | loop fusion | flops 4194304 | bytes 12582912 | tf_op jit(solution)/shard_map/convert_element_type | solution.py:122
  (127 shorter events, 26.4 us)
Async XLA Ops:
  0.6 70.4 %copy-start = (bf16[3,3,3,256,256]{4,3,2,1,0:T(8,128)(2,1)S(1)}, bf16[3,3,3,256,256]{4,3,2,1,0:T(8,128)(2,1)}, u32[]{:S(2)}) copy-start(bf16[3,3,3,256,256]{4,3,2,1,0:T(8,128)(2,1)} %param.7) | copy-start | bytes 10616836
  2.1 0.6 copy-start.9
  4.8 44.0 %collective-permute-start = (bf16[2,4,128,256]{3,2,1,0:T(8,128)(2,1)}, bf16[2,4,128,256]{3,2,1,0:T(8,128)(2,1)}, u32[]{:S(2)}, u32[]{:S(2)}) collective-permute-start(bf16[2,4,128,256]{3,2,1,0:T(8,128)(2,1)} %fusion.21), channel_id=1, source_target_pairs={{0,4},{4,8},{8,12},{12,16},{16,20},{20,24},{24,28},{1,5},{5,9},{9,... | collective-permute-start | bytes 1572872 | tf_op jit(solution)/shard_map/ppermute | solution.py:12
  34.3 0.6 copy-start.11
  34.9 0.6 copy-start.12
  36.2 5.2 %copy-start.14 = (s32[1024,1]{0,1:T(1,128)}, s32[1024,1]{0,1:T(1,128)S(1)}, u32[]{:S(2)}) copy-start(s32[1024,1]{0,1:T(1,128)S(1)} %compare_select_fusion.3) | copy-start | bytes 12292
  41.4 16.1 %all-to-all-start = ((s32[32,1,64]{2,1,0:T(1,128)}), s32[32,1,64]{2,1,0:T(1,128)S(1)}, u32[]{:S(2)}, u32[]{:S(2)}) async-start(s32[32,1,64]{2,1,0:T(1,128)} %all_to_all.12), calls=%async_computation | async-start | bytes 32768 | tf_op jit(solution)/shard_map/all_to_all | solution.py:86
  50.7 8.7 %collective-permute-start.1 = (bf16[4,1,128,256]{3,2,1,0:T(8,128)(2,1)}, bf16[4,1,128,256]{3,2,1,0:T(8,128)(2,1)}, u32[]{:S(2)}, u32[]{:S(2)}) collective-permute-start(bf16[4,1,128,256]{3,2,1,0:T(8,128)(2,1)} %get-tuple-element.11), channel_id=1, source_target_pairs={{0,1},{1,2},{2,3},{4,5},{5,6},{6,7},{8,9},{9,10},{10,11},{12,13},{... | collective-permute-start | bytes 786440 | tf_op jit(solution)/shard_map/ppermute | solution.py:20
  54.3 8.0 %collective-permute-start.2 = (bf16[4,1,128,256]{3,2,1,0:T(8,128)(2,1)}, bf16[4,1,128,256]{3,2,1,0:T(8,128)(2,1)}, u32[]{:S(2)}, u32[]{:S(2)}) collective-permute-start(bf16[4,1,128,256]{3,2,1,0:T(8,128)(2,1)} %get-tuple-element.12), channel_id=1, source_target_pairs={{1,0},{2,1},{3,2},{5,4},{6,5},{7,6},{9,8},{10,9},{11,10},{13,12},{... | collective-permute-start | bytes 786440 | tf_op jit(solution)/shard_map/ppermute | solution.py:23
  64.4 5.8 %copy-start.6 = (bf16[2,4,128,256]{3,2,1,0:T(8,128)(2,1)S(1)}, bf16[2,4,128,256]{3,2,1,0:T(8,128)(2,1)}, u32[]{:S(2)}) copy-start(bf16[2,4,128,256]{3,2,1,0:T(8,128)(2,1)} %param.6) | copy-start | bytes 1572868
  64.4 5.8 %copy-start.10 = (f32[2,4,128]{2,1,0:T(4,128)S(1)}, f32[2,4,128]{2,1,0:T(4,128)}, u32[]{:S(2)}) copy-start(f32[2,4,128]{2,1,0:T(4,128)} %copy-done.9) | copy-start | bytes 12292
  71.0 7.4 %copy-start.13 = (s32[2048]{0:T(1024)S(1)}, s32[2048]{0:T(1024)}, u32[]{:S(2)}) copy-start(s32[2048]{0:T(1024)} %reshape.472) | copy-start | bytes 24580
  74.9 3.5 %copy-start.7 = (bf16[2,4,128,256]{3,2,1,0:T(8,128)(2,1)}, bf16[2,4,128,256]{3,2,1,0:T(8,128)(2,1)S(1)}, u32[]{:S(2)}) copy-start(bf16[2,4,128,256]{3,2,1,0:T(8,128)(2,1)S(1)} %get-tuple-element.18) | copy-start | bytes 1572868
  75.3 27.0 %collective-permute-start.3 = (bf16[2,4,128,256]{3,2,1,0:T(8,128)(2,1)S(1)}, bf16[2,4,128,256]{3,2,1,0:T(8,128)(2,1)S(1)}, u32[]{:S(2)}, u32[]{:S(2)}) collective-permute-start(bf16[2,4,128,256]{3,2,1,0:T(8,128)(2,1)S(1)} %fusion.17), channel_id=1, source_target_pairs={{0,4},{4,8},{8,12},{12,16},{16,20},{20,24},{24,28},{1,5},{5,9},{9,... | collective-permute-start | bytes 1572872 | tf_op jit(solution)/shard_map/ppermute | solution.py:12
  102.3 36.5 %copy-start.2 = (bf16[2,4,128,256]{3,2,1,0:T(8,128)(2,1)}, bf16[2,4,128,256]{3,2,1,0:T(8,128)(2,1)S(1)}, u32[]{:S(2)}) copy-start(bf16[2,4,128,256]{3,2,1,0:T(8,128)(2,1)S(1)} %collective-permute-done.3) | copy-start | bytes 1572868
  102.3 50.8 %collective-permute-start.4 = (bf16[4,1,128,256]{3,2,1,0:T(8,128)(2,1)S(1)}, bf16[4,1,128,256]{3,2,1,0:T(8,128)(2,1)S(1)}, u32[]{:S(2)}, u32[]{:S(2)}) collective-permute-start(bf16[4,1,128,256]{3,2,1,0:T(8,128)(2,1)S(1)} %get-tuple-element.7), channel_id=1, source_target_pairs={{0,1},{1,2},{2,3},{4,5},{5,6},{6,7},{8,9},{9,10},{10,11},{12,13},{... | collective-permute-start | bytes 786440 | tf_op jit(solution)/shard_map/ppermute | solution.py:20
  135.4 17.8 %collective-permute-start.5 = (bf16[4,1,128,256]{3,2,1,0:T(8,128)(2,1)S(1)}, bf16[4,1,128,256]{3,2,1,0:T(8,128)(2,1)}, u32[]{:S(2)}, u32[]{:S(2)}) collective-permute-start(bf16[4,1,128,256]{3,2,1,0:T(8,128)(2,1)S(1)} %get-tuple-element.8), channel_id=1, source_target_pairs={{1,0},{2,1},{3,2},{5,4},{6,5},{7,6},{9,8},{10,9},{11,10},{13,12},{... | collective-permute-start | bytes 786440 | tf_op jit(solution)/shard_map/ppermute | solution.py:23
  138.8 39.7 %all-to-all-start.1 = ((bf16[32,64,256]{2,1,0:T(8,128)(2,1)}), bf16[32,64,256]{2,1,0:T(8,128)(2,1)S(1)}, u32[]{:S(2)}, u32[]{:S(2)}) async-start(bf16[32,64,256]{2,1,0:T(8,128)(2,1)} %select_select_fusion), calls=%async_computation.1 | async-start | bytes 2097152 | tf_op jit(solution)/shard_map/all_to_all | solution.py:97
  153.2 5.9 %copy-start.3 = (bf16[2,4,128,256]{3,2,1,0:T(8,128)(2,1)S(1)}, bf16[2,4,128,256]{3,2,1,0:T(8,128)(2,1)}, u32[]{:S(2)}) copy-start(bf16[2,4,128,256]{3,2,1,0:T(8,128)(2,1)} %copy-done.2) | copy-start | bytes 1572868
  155.3 4.5 %copy-start.8 = (bf16[2,4,128,256]{3,2,1,0:T(8,128)(2,1)S(1)}, bf16[2,4,128,256]{3,2,1,0:T(8,128)(2,1)}, u32[]{:S(2)}) copy-start(bf16[2,4,128,256]{3,2,1,0:T(8,128)(2,1)} %copy-done.7) | copy-start | bytes 1572868
  157.0 3.5 %copy-start.17 = (bf16[3,3,3,256,256]{4,3,2,1,0:T(8,128)(2,1)S(1)}, bf16[3,3,3,256,256]{4,3,2,1,0:T(8,128)(2,1)}, u32[]{:S(2)}) copy-start(bf16[3,3,3,256,256]{4,3,2,1,0:T(8,128)(2,1)} %param.8) | copy-start | bytes 10616836
  160.3 18.2 %copy-start.15 = (s32[1024]{0:T(1024)S(1)}, s32[1024]{0:T(1024)}, u32[]{:S(2)}) copy-start(s32[1024]{0:T(1024)} %broadcast_clamp_fusion.1) | copy-start | bytes 12292
  160.5 22.0 %copy-start.16 = (pred[1024]{0:T(1024)(128)(4,1)S(1)}, pred[1024]{0:T(1024)(128)(4,1)}, u32[]{:S(2)}) copy-start(pred[1024]{0:T(1024)(128)(4,1)} %compare_and_fusion.2) | copy-start | bytes 3076
  165.0 17.4 %copy-start.4 = (f32[2,4,128,256]{3,2,1,0:T(8,128)}, f32[2,4,128,256]{3,2,1,0:T(8,128)S(1)}, u32[]{:S(2)}) copy-start(f32[2,4,128,256]{3,2,1,0:T(8,128)S(1)} %get-tuple-element.20) | copy-start | bytes 3145732
  182.4 1.0 copy-start.5
  189.6 50.8 %copy-start.1 = (bf16[3,3,3,256,256]{4,3,2,1,0:T(8,128)(2,1)S(1)}, bf16[3,3,3,256,256]{4,3,2,1,0:T(8,128)(2,1)}, u32[]{:S(2)}) copy-start(bf16[3,3,3,256,256]{4,3,2,1,0:T(8,128)(2,1)} %param.7) | copy-start | bytes 10616836
  189.6 30.0 %all-to-all-start.2 = ((bf16[32,64,256]{2,1,0:T(8,128)(2,1)}), bf16[32,64,256]{2,1,0:T(8,128)(2,1)}, u32[]{:S(2)}, u32[]{:S(2)}) async-start(bf16[32,64,256]{2,1,0:T(8,128)(2,1)} %bitcast.64), calls=%async_computation.2 | async-start | bytes 2097152 | tf_op jit(solution)/shard_map/all_to_all | solution.py:107
where the time goes:
time: 242 us; the launch traced here: 240 us
  other arithmetic  72.1 us (30%)
  starting transfers between devices  72 us (30%)
  local copies, waits for them, and re-layouts  52.7 us (22%)
  waiting for transfers between devices  33.7 us (14%)
  matrix products  8.41 us (3%)
    ppermute x2, starting transfers between devices, extended_2(): lax.ppermute(lax.slice_in_dim(block, block.shape[dim] - width, None, axis...  36.6 us
    gather x1, local copies, waits for them, and re-layouts, on_device(): found_rows = jnp.take(codebook, local_rows, axis=0)  23.8 us
    another operation x3, other arithmetic  18.5 us
    all_to_all x1, waiting for transfers between devices, on_device(): lax.all_to_all(term_slots.reshape(owners, capacity, channels), ('tm', 'he...  17.4 us
    scatter-add x1, other arithmetic, on_device(): sums = jnp.zeros((range_rows, channels), jnp.float32).at[target_rows.resh...  14.6 us
    all_to_all x1, starting transfers between devices, on_device(): lax.all_to_all(found_rows, ('tm', 'height'), split_axis=0, concat_axis=0,...  14.3 us
    all_to_all x1, waiting for transfers between devices, on_device(): lax.all_to_all(found_rows, ('tm', 'height'), split_axis=0, concat_axis=0,...  13.5 us
    dot_general x2, matrix products, conv_block(): jnp.dot(patch, weight.reshape(27 * channels, channels), preferred_element...  8.41 us
  transfers between devices with their start and end apart: 9, of which 3 were waited for; matrix products, arithmetic and copies ran while one was open for 34% of the time, Pallas kernels for 0%

commit v1 on v0

v1 whole, which is shorter than its diff:
```python
import functools

import jax
import jax.numpy as jnp
from jax import lax
from jax.experimental import pallas as pl
from jax.experimental.pallas import tpu as pltpu
from jax.sharding import PartitionSpec as P

COMMIT = 0.25
BATCH = 64
TILE = 16
F32 = jnp.float32
BF16 = jnp.bfloat16
VMEM = pl.BlockSpec(memory_space=pltpu.VMEM)
SMEM = pl.BlockSpec(memory_space=pltpu.SMEM)
HBM = pl.BlockSpec(memory_space=pl.ANY)
NT = (((1,), (1,)), ((), ()))


def along(x, axis, by):
    count = lax.axis_size(axis)
    return lax.ppermute(x, axis, [(i, i + by) for i in range(count) if 0 <= i + by < count])


def around(x, axis, by):
    count = lax.axis_size(axis)
    return lax.ppermute(x, axis, [(i, (i + by) % count) for i in range(count)])


def params(megabytes):
    return pltpu.CompilerParams(vmem_limit_bytes=megabytes << 20)


def act(values):
    scaled = values * lax.rsqrt(jnp.mean(values * values, -1, keepdims=True) + 1e-06)
    return scaled / (1.0 + jnp.exp(-scaled))


def lanes(block):
    return jnp.concatenate([block[i : i + 1, :] for i in range(block.shape[0])], axis=1)


def onehot(mask):
    return jnp.where(mask, 1.0, 0.0).astype(BF16)


def index_kernel(groups, tiles, held, capacity, where_ref, codes_ref, ask_ref, low_ref, send_ref, place_ref):
    lines, width = codes_ref.shape[1:]
    cells = lines * width
    owners = groups * tiles
    range_rows = held // tiles
    block_slots = tiles * capacity
    batches = block_slots // BATCH
    here = where_ref[0]
    own = lanes(codes_ref[here])
    block = own // range_rows
    target = block % tiles * groups + block // tiles
    home = own // held
    arrival = lax.rem(here - home + groups, groups)
    peers = [lanes(codes_ref[lax.rem(here + k, groups)]) for k in range(groups)]
    own_hits = lax.broadcasted_iota(jnp.int32, (owners, cells), 0) == target
    home_hits = lax.broadcasted_iota(jnp.int32, (groups, cells), 0) == arrival
    peer_hits = [peer // held == here for peer in peers]
    hits = jnp.concatenate(
        [jnp.where(own_hits, 1.0, 0.0), jnp.where(home_hits, 1.0, 0.0)] + [jnp.where(x, 1.0, 0.0) for x in peer_hits], axis=0
    )
    count = hits.shape[0]
    pad = -count % 16
    if pad:
        hits = jnp.concatenate([hits, jnp.zeros((pad, cells), F32)], axis=0)
    earlier = onehot(
        lax.broadcasted_iota(jnp.int32, (width, width), 0) < lax.broadcasted_iota(jnp.int32, (width, width), 1)
    )
    before = jnp.zeros((count + pad, 1), F32)
    parts = []
    for i in range(lines):
        part = hits[:, i * width : (i + 1) * width]
        parts.append(jnp.dot(part.astype(BF16), earlier, preferred_element_type=F32) + before)
        before = before + jnp.sum(part, 1, keepdims=True)
    ranks = jnp.concatenate(parts, axis=1)
    own_rank = jnp.sum(ranks[:owners] * hits[:owners], 0, keepdims=True)
    home_rank = jnp.sum(ranks[owners : owners + groups] * hits[owners : owners + groups], 0, keepdims=True)
    place_ref[0:1, :] = target.astype(F32) * capacity + own_rank
    place_ref[1:2, :] = arrival.astype(F32) * block_slots + home_rank
    place_ref[2:, :] = jnp.zeros((6, cells), F32)
    local = own % range_rows
    own_ones = hits[:owners]
    picked = jnp.concatenate(
        [own_ones * (local // 256).astype(F32), own_ones * (local % 256).astype(F32), own_ones], axis=0
    ).astype(BF16)
    chosen = onehot(lax.broadcasted_iota(jnp.int32, (capacity, cells), 0).astype(F32) == own_rank)
    slots = lax.dot_general(picked, chosen, NT, preferred_element_type=F32)
    code = slots[:owners] * 256.0 + slots[owners : 2 * owners]
    send_ref[...] = jnp.where(slots[2 * owners :] > 0.5, code, -1.0).astype(jnp.int32)
    columns = []
    for k in range(groups):
        hit = hits[owners + groups + k : owners + groups + k + 1]
        rank = ranks[owners + groups + k : owners + groups + k + 1].astype(jnp.int32)
        row = jnp.where(peer_hits[k], peers[k] - here * held, 0)
        batch = onehot(
            lax.broadcasted_iota(jnp.int32, (batches, cells), 0) == jnp.where(peer_hits[k], rank // BATCH, -1)
        ).astype(F32)
        tile = row // TILE
        picked = jnp.concatenate(
            [
                batch * (tile // 128).astype(F32),
                batch * (tile % 128).astype(F32),
                batch,
                batch * (row % TILE).astype(F32),
            ],
            axis=0,
        ).astype(BF16)
        chosen = onehot(lax.broadcasted_iota(jnp.int32, (BATCH, cells), 0) == rank % BATCH)
        slots = lax.dot_general(picked, chosen, NT, preferred_element_type=F32)
        asked = slots[:batches] * 128.0 + slots[batches : 2 * batches]
        ask_ref[k * batches : (k + 1) * batches, :] = jnp.where(
            slots[2 * batches : 3 * batches] > 0.5, asked, -1.0
        ).astype(jnp.int32)
        columns.append(lax.dot_general(chosen, picked[3 * batches :], NT, preferred_element_type=F32))
    low_ref[...] = jnp.concatenate(columns, axis=1)


def gather_kernel(batches, ask_ref, book_ref, low_ref, *refs):
    outs, land, sems = refs[:-2], refs[-2], refs[-1]
    total = len(outs) * batches

    def copy_in(g):
        def one(i, carry):
            tile = jnp.maximum(ask_ref[g, i], 0)
            pltpu.make_async_copy(book_ref.at[tile], land.at[g * BATCH + i], sems.at[g]).start()
            return carry

        lax.fori_loop(0, BATCH, one, 0, unroll=16)

    for g in range(total):
        pl.when(ask_ref[g, 0] >= 0)(functools.partial(copy_in, g))
    at = lax.broadcasted_iota(jnp.int32, (BATCH, BATCH * TILE), 1)
    at = at - TILE * lax.broadcasted_iota(jnp.int32, (BATCH, BATCH * TILE), 0)
    at = at.astype(F32)
    for g in range(total):
        out = outs[g // batches]
        span = slice(g % batches * BATCH, (g % batches + 1) * BATCH)
        filled = ask_ref[g, 0] >= 0

        @pl.when(filled)
        def _(g=g, out=out, span=span):
            block = land.at[pl.ds(g * BATCH, BATCH)]
            pltpu.make_async_copy(book_ref.at[pl.ds(0, BATCH)], block, sems.at[g]).wait()
            tiles = land[g * BATCH : (g + 1) * BATCH].reshape(BATCH * TILE, land.shape[-1])
            out[span, :] = jnp.dot(onehot(at == low_ref[:, g : g + 1]), tiles, preferred_element_type=F32).astype(BF16)

        @pl.when(jnp.logical_not(filled))
        def _(out=out, span=span):
            out[span, :] = jnp.zeros((BATCH, out.shape[-1]), BF16)


def convolve(window, weight_ref, frame):
    rows, columns, channels = window.shape[1] - 2, window.shape[2], window.shape[3]
    flat = rows * columns
    pieces = [window[frame + p, q : q + rows].reshape(flat, channels) for p in range(3) for q in range(3)]
    patch = jnp.concatenate(pieces, axis=1)
    place = lax.broadcasted_iota(jnp.int32, (flat, 1), 0) % columns
    sums = [
        jnp.dot(patch, weight_ref[:, :, r].reshape(9 * channels, channels), preferred_element_type=F32)
        for r in range(3)
    ]
    left = jnp.where(place == 0, 0.0, pltpu.roll(sums[0], 1, 0))
    right = jnp.where(place == columns - 1, 0.0, pltpu.roll(sums[2], flat - 1, 0))
    return sums[1] + left + right


def fill_window(window, own, before, sides, corners, change):
    window[0:2, 1:2] = change(before[0][...])
    window[0:2, 2:-2] = change(before[1][...])
    window[0:2, -2:-1] = change(before[2][...])
    window[0:2, 0:1] = change(corners[0][...])
    window[0:2, -1:] = change(corners[1][...])
    window[2:4, 0:1] = change(sides[0][...])
    window[2:4, -1:] = change(sides[1][...])
    if len(own) == 1:
        window[2:4, 1:-1] = change(own[0][...])
    else:
        window[2:4, 1:2] = change(own[0][...])
        window[2:4, 2:-2] = change(own[1][...])
        window[2:4, -2:-1] = change(own[2][...])


def first_kernel(video, b0, b1, b2, s0, s1, c0, c1, weight, first, top, mid, bottom, window):
    fill_window(window, (video,), (b0, b1, b2), (s0, s1), (c0, c1), lambda x: act(x.astype(F32)).astype(BF16))
    frames, rows, columns, channels = video.shape
    for f in range(frames):
        conv = convolve(window, weight, f).reshape(rows, columns, channels)
        result = (video[f].astype(F32) + conv).astype(BF16)
        first[f] = result
        active = act(result.astype(F32)).astype(BF16)
        top[f] = active[0:1]
        mid[f] = active[1:-1]
        bottom[f] = active[-1:]


def second_kernel(
    first, o0, o1, o2, b0, b1, b2, s0, s1, c0, c1, weight, place, quant_slots, encoded, terms, window
):
    fill_window(window, (o0, o1, o2), (b0, b1, b2), (s0, s1), (c0, c1), lambda x: x)
    frames, rows, columns, channels = first.shape
    for f in range(frames):
        conv = convolve(window, weight, f).reshape(rows, columns, channels)
        encoded[f] = (first[f].astype(F32) + conv).astype(BF16)
    flat = encoded[...].reshape(frames * rows * columns, channels)
    cells = flat.shape[0]
    slots = quant_slots.shape[0]
    step = 256
    for i in range(slots // step):
        mine = lax.broadcasted_iota(jnp.int32, (step, cells), 0).astype(F32) + float(i * step) == place[0:1, :]
        packed = jnp.dot(onehot(mine), flat, preferred_element_type=F32)
        span = slice(i * step, (i + 1) * step)
        terms[span, :] = (quant_slots[span, :].astype(F32) - packed).astype(BF16)


def quant_kernel(place, *refs):
    parts, quant, quant_slots = refs[:-2], refs[-2], refs[-1]
    cells = quant.shape[0]
    part_slots = parts[0].shape[0]
    column = place[...].T[:, 1:2]
    step = 256
    for i in range(cells // step):
        total = jnp.zeros((step, quant.shape[1]), F32)
        for k, part in enumerate(parts):
            at = lax.broadcasted_iota(jnp.int32, (step, part_slots), 1).astype(F32) + float(k * part_slots)
            mine = onehot(at == column[i * step : (i + 1) * step])
            total = total + jnp.dot(mine, part[...], preferred_element_type=F32)
        quant[i * step : (i + 1) * step, :] = total.astype(BF16)
    rows = quant[...]
    for i in range(quant_slots.shape[0] // step):
        mine = lax.broadcasted_iota(jnp.int32, (step, cells), 0).astype(F32) + float(i * step) == place[0:1, :]
        quant_slots[i * step : (i + 1) * step, :] = jnp.dot(onehot(mine), rows, preferred_element_type=F32).astype(BF16)


def rotate_kernel(encoded, quant, upstream, out):
    step = 128

    def one(i, carry):
        span = pl.ds(pl.multiple_of(i * step, step), step)
        e = encoded[span, :].astype(F32)
        q = quant[span, :].astype(F32)
        g = upstream[span, :].astype(F32)
        lat_norm = jnp.sqrt(jnp.sum(e * e, -1, keepdims=True) + 1e-06)
        quant_norm = jnp.sqrt(jnp.sum(q * q, -1, keepdims=True) + 1e-06)
        a = e / lat_norm
        b = q / quant_norm
        cosine = jnp.sum(a * b, -1, keepdims=True)
        s = a + b
        turned = g - s * (jnp.sum(s * g, -1, keepdims=True) / (1.0 + cosine))
        turned = turned + 2.0 * a * jnp.sum(b * g, -1, keepdims=True)
        out[span, :] = (quant_norm / lat_norm * turned + 2.0 * COMMIT * (e - q)).astype(BF16)
        return carry

    lax.fori_loop(0, encoded.shape[0] // step, one, 0)


def scatter_kernel(target, terms, out):
    rows, slots = out.shape[0], terms.shape[0]
    at = lax.broadcasted_iota(jnp.int32, (rows, slots), 0) + pl.program_id(0) * rows
    sums = jnp.dot(onehot(at == target[...]), terms[...], preferred_element_type=F32)
    out[...] = (2.0 * sums).astype(BF16)


def halo(top, mid, bottom):
    b_top = along(top, "tm", 1)
    b_bottom = along(bottom, "tm", 1)
    up = along(bottom, "height", 1)
    down = along(top, "height", -1)
    b_mid = along(mid, "tm", 1)
    corner_up = along(b_bottom, "height", 1)
    corner_down = along(b_top, "height", -1)
    return b_top, b_mid, b_bottom, up, down, corner_up, corner_down


def on_device(latents, conv_first, conv_second, codebook, codes, upstream):
    frames, rows, columns, channels = latents.shape
    cells = frames * rows * columns
    held = codebook.shape[0]
    tiles = lax.axis_size("tm")
    groups = lax.axis_size("height")
    owners = tiles * groups
    range_rows = held // tiles
    capacity = 2 * cells // owners
    slots = owners * capacity
    block_slots = slots // groups
    video = jax.ShapeDtypeStruct((frames, rows, columns, channels), BF16)
    edge = jax.ShapeDtypeStruct((frames, 1, columns, channels), BF16)
    inner = jax.ShapeDtypeStruct((frames, rows - 2, columns, channels), BF16)

    halo_one = halo(latents[:, :1], latents[:, 1:-1], latents[:, -1:])

    where = lax.axis_index("height").astype(jnp.int32).reshape(1)
    shared = lax.all_gather(codes.reshape(frames * rows, columns), "height")
    ask, low, send, place = pl.pallas_call(
        functools.partial(index_kernel, groups, tiles, held, capacity),
        out_shape=(
            jax.ShapeDtypeStruct((slots // BATCH, BATCH), jnp.int32),
            jax.ShapeDtypeStruct((BATCH, slots // BATCH), F32),
            jax.ShapeDtypeStruct((owners, capacity), jnp.int32),
            jax.ShapeDtypeStruct((8, cells), F32),
        ),
        in_specs=[SMEM, VMEM],
        out_specs=(VMEM,) * 4,
        compiler_params=params(32),
    )(where, shared)
    found = pl.pallas_call(
        functools.partial(gather_kernel, block_slots // BATCH),
        out_shape=(jax.ShapeDtypeStruct((block_slots, channels), BF16),) * groups,
        in_specs=[SMEM, HBM, VMEM],
        out_specs=(VMEM,) * groups,
        scratch_shapes=[
            pltpu.VMEM((slots, TILE, channels), BF16),
            pltpu.SemaphoreType.DMA((slots // BATCH,)),
        ],
        compiler_params=params(40),
    )(ask, codebook.reshape(held // TILE, TILE, channels), low)
    asked = [found[0]] + [around(found[k], "height", k) for k in range(1, groups)]
    owner_codes = lax.all_to_all(send, ("tm", "height"), split_axis=0, concat_axis=0, tiled=True)

    first, top, mid, bottom = pl.pallas_call(
        first_kernel,
        out_shape=(video, edge, inner, edge),
        in_specs=[VMEM] * 9,
        out_specs=(VMEM,) * 4,
        scratch_shapes=[pltpu.VMEM((frames + 2, rows + 2, columns, channels), BF16)],
        compiler_params=params(40),
    )(latents, *halo_one, conv_first)
    halo_two = halo(top, mid, bottom)

    quant, quant_slots = pl.pallas_call(
        quant_kernel,
        out_shape=(
            jax.ShapeDtypeStruct((cells, channels), BF16),
            jax.ShapeDtypeStruct((slots, channels), BF16),
        ),
        in_specs=[VMEM] * (1 + groups),
        out_specs=(VMEM,) * 2,
        compiler_params=params(32),
    )(place, *asked)

    encoded, terms = pl.pallas_call(
        second_kernel,
        out_shape=(video, jax.ShapeDtypeStruct((slots, channels), BF16)),
        in_specs=[VMEM] * 14,
        out_specs=(VMEM,) * 2,
        scratch_shapes=[pltpu.VMEM((frames + 2, rows + 2, columns, channels), BF16)],
        compiler_params=params(40),
    )(first, top, mid, bottom, *halo_two, conv_second, place, quant_slots)
    owner_terms = lax.all_to_all(
        terms.reshape(owners, capacity, channels), ("tm", "height"), split_axis=0, concat_axis=0, tiled=True
    )
    grad_flat = pl.pallas_call(
        rotate_kernel,
        out_shape=jax.ShapeDtypeStruct((cells, channels), BF16),
        in_specs=[VMEM] * 3,
        out_specs=VMEM,
        compiler_params=params(16),
    )(encoded.reshape(cells, channels), quant, upstream.reshape(cells, channels))
    step = 256
    codebook_grad = pl.pallas_call(
        scatter_kernel,
        grid=(range_rows // step,),
        out_shape=jax.ShapeDtypeStruct((range_rows, channels), BF16),
        in_specs=[
            pl.BlockSpec((1, slots), lambda i: (0, 0)),
            pl.BlockSpec((slots, channels), lambda i: (0, 0)),
        ],
        out_specs=pl.BlockSpec((step, channels), lambda i: (i, 0)),
        compiler_params=params(32),
    )(owner_codes.reshape(1, slots), owner_terms.reshape(slots, channels))
    return (grad_flat.reshape(upstream.shape), codebook_grad)


def solution(mesh):
    return jax.shard_map(
        on_device,
        mesh=mesh,
        in_specs=(
            P("tm", "height", None, None),
            P(),
            P(),
            P("height", None),
            P("tm", "height", None),
            P("tm", "height", None, None),
        ),
        out_specs=(P("tm", "height", None, None), P(("height", "tm"), None)),
        check_vma=False,
    )
```

time: 242 us -> 154 us (0.64)
  other arithmetic: 72.1 us -> 0.73 us
  Pallas kernels: 0 us -> 49.3 us
  local copies, waits for them, and re-layouts: 52.7 us -> 20.3 us
  starting transfers between devices: 72 us -> 53.4 us
  waiting for transfers between devices: 33.7 us -> 21.4 us
  matrix products: 8.41 us -> 0 us
  blocking collectives: 0 us -> 5.85 us
    pallas_call x0 -> x7, Pallas kernels: none -> 49.3 us  [the longest x1 18 us: on_device(): pl.pallas_call(scatter_kernel, grid=(range_rows // step,), out_shape=jax....]
    gather x2 -> x0, local copies, waits for them, and re-layouts: 27.7 us -> none  [the longest x1 23.8 us: on_device(): found_rows = jnp.take(codebook, local_rows, axis=0)]
    another operation x3 -> x0, other arithmetic: 18.5 us -> none
    all_to_all x3 -> x2, starting transfers between devices: 23.7 us -> 7.67 us  [the longest x1 5.22 us: on_device(): lax.all_to_all(terms.reshape(owners, capacity, channels), ('tm', 'height'...]
    scatter-add x1 -> x0, other arithmetic: 14.6 us -> none  [on_device(): sums = jnp.zeros((range_rows, channels), jnp.float32).at[target_rows.resh...]
    convert_element_type x6 -> x0, other arithmetic: 13.3 us -> none  [the longest x1 6.13 us: on_device(): return (grad_latent, (2.0 * sums).astype(jnp.bfloat16))]
    all_to_all x3 -> x2, waiting for transfers between devices: 30.9 us -> 17.7 us  [the longest x1 17.7 us: on_device(): lax.all_to_all(terms.reshape(owners, capacity, channels), ('tm', 'height'...]
    scatter x2 -> x0, local copies, waits for them, and re-layouts: 10.6 us -> none  [the longest x1 6.13 us: on_device(): jnp.zeros((owners * capacity, channels), jnp.bfloat16).at[slot_index]]
  transfers between devices with their start and end apart: 9 -> 19, of which waited for: 3 -> 2; matrix products, arithmetic and copies ran while one was open for 34% -> 2% of each run, Pallas kernels for 0% -> 21%
where the time goes in v1:
time: 154 us; the launch traced here: 152 us
  starting transfers between devices  53.4 us (35%)
  Pallas kernels  49.3 us (32%)
  waiting for transfers between devices  21.4 us (14%)
  local copies, waits for them, and re-layouts  20.3 us (13%)
  blocking collectives  5.85 us (4%)
    ppermute x14, starting transfers between devices, along(): lax.ppermute(x, axis, [(i, i + by) for i in range(count) if 0 <= i + by <...  43.8 us
    pallas_call x1, Pallas kernels, on_device(): pl.pallas_call(scatter_kernel, grid=(range_rows // step,), out_shape=jax....  18 us
    all_to_all x1, waiting for transfers between devices, on_device(): lax.all_to_all(terms.reshape(owners, capacity, channels), ('tm', 'height'...  17.7 us
    unnamed x44, local copies, waits for them, and re-layouts  16.3 us
    pallas_call x1, Pallas kernels, on_device(): pl.pallas_call(functools.partial(gather_kernel, block_slots // BATCH), ou...  11.8 us
    pallas_call x1, Pallas kernels, on_device(): pl.pallas_call(second_kernel, out_shape=(video, jax.ShapeDtypeStruct((slo...  6.32 us
    pallas_call x1, Pallas kernels, on_device(): pl.pallas_call(first_kernel, out_shape=(video, edge, inner, edge), in_spe...  6.08 us
    all_gather x1, blocking collectives, on_device(): shared = lax.all_gather(codes.reshape(frames * rows, columns), 'height')  5.85 us
  transfers between devices with their start and end apart: 19, of which 2 were waited for; matrix products, arithmetic and copies ran while one was open for 2% of the time, Pallas kernels for 21%

profile of v1, /device:TPU:1, one launch (start us, length us, event | category | flops | bytes accessed | tf_op | source)
XLA Modules:
  0.0 152.0 jit_solution(14925314671649157700)
XLA Ops:
  0.6 1.7 %fusion = (bf16[2,1,128,256]{3,2,1,0:T(8,128)(2,1)}, bf16[2,1,128,256]{3,2,1,0:T(8,128)(2,1)}) fusion(bf16[2,4,128,256]{3,2,1,0:T(8,128)(2,1)} %video.1), kind=kLoop, calls=%fused_computation | loop fusion | bytes 524288 | tf_op jit(solution)/shard_map/slice | solution.py:295
  2.3 4.6 %collective-permute-start.2 = (bf16[2,1,128,256]{3,2,1,0:T(8,128)(2,1)}, bf16[2,1,128,256]{3,2,1,0:T(8,128)(2,1)}, u32[]{:S(2)}, u32[]{:S(2)}) collective-permute-start(bf16[2,1,128,256]{3,2,1,0:T(8,128)(2,1)} %get-tuple-element.34), channel_id=1, source_target_pairs={{0,4},{4,8},{8,12},{12,16},{16,20},{20,24},{24,28},{1,5},{5,9},{9,... | collective-permute-start | bytes 393224 | tf_op jit(solution)/shard_map/ppermute | solution.py:23
  6.9 3.9 %collective-permute-start.3 = (bf16[2,1,128,256]{3,2,1,0:T(8,128)(2,1)}, bf16[2,1,128,256]{3,2,1,0:T(8,128)(2,1)}, u32[]{:S(2)}, u32[]{:S(2)}) collective-permute-start(bf16[2,1,128,256]{3,2,1,0:T(8,128)(2,1)} %get-tuple-element.34), channel_id=1, source_target_pairs={{0,1},{1,2},{2,3},{4,5},{5,6},{6,7},{8,9},{9,10},{10,11},{12,13},{... | collective-permute-start | bytes 393224 | tf_op jit(solution)/shard_map/ppermute | solution.py:23
  10.9 1.9 %collective-permute-start.4 = (bf16[2,1,128,256]{3,2,1,0:T(8,128)(2,1)}, bf16[2,1,128,256]{3,2,1,0:T(8,128)(2,1)}, u32[]{:S(2)}, u32[]{:S(2)}) collective-permute-start(bf16[2,1,128,256]{3,2,1,0:T(8,128)(2,1)} %get-tuple-element.35), channel_id=1, source_target_pairs={{1,0},{2,1},{3,2},{5,4},{6,5},{7,6},{9,8},{10,9},{11,10},{13,12},{... | collective-permute-start | bytes 393224 | tf_op jit(solution)/shard_map/ppermute | solution.py:23
  12.8 3.2 %collective-permute-start = (bf16[2,1,128,256]{3,2,1,0:T(8,128)(2,1)}, bf16[2,1,128,256]{3,2,1,0:T(8,128)(2,1)}, u32[]{:S(2)}, u32[]{:S(2)}) collective-permute-start(bf16[2,1,128,256]{3,2,1,0:T(8,128)(2,1)} %get-tuple-element.35), channel_id=1, source_target_pairs={{0,4},{4,8},{8,12},{12,16},{16,20},{20,24},{24,28},{1,5},{5,9},{9,... | collective-permute-start | bytes 393224 | tf_op jit(solution)/shard_map/ppermute | solution.py:23
  16.0 1.7 %slice.10 = bf16[2,2,128,256]{3,2,1,0:T(8,128)(2,1)} slice(bf16[2,4,128,256]{3,2,1,0:T(8,128)(2,1)} %video.1), slice={[0:2], [1:3], [0:128], [0:256]} | slice | bytes 524288 | tf_op jit(solution)/shard_map/slice | solution.py:295
  17.7 3.2 %collective-permute-start.1 = (bf16[2,2,128,256]{3,2,1,0:T(8,128)(2,1)}, bf16[2,2,128,256]{3,2,1,0:T(8,128)(2,1)}, u32[]{:S(2)}, u32[]{:S(2)}) collective-permute-start(bf16[2,2,128,256]{3,2,1,0:T(8,128)(2,1)} %slice.10), channel_id=1, source_target_pairs={{0,4},{4,8},{8,12},{12,16},{16,20},{20,24},{24,28},{1,5},{5,9},{9,... | collective-permute-start | bytes 786440 | tf_op jit(solution)/shard_map/ppermute | solution.py:23
  20.9 5.9 %all_gather.3.codes_ref = s32[4,8,128]{2,1,0:T(8,128)S(1)} all-gather(s32[1,8,128]{2,1,0:T(8,128)} %bitcast.17), channel_id=1, replica_groups=mesh['tm'=8,'height'=4] {'height'}, dimensions={0}, use_global_device_ids=true | all-gather | bytes 20480 | tf_op jit(solution)/shard_map/all_gather | solution.py:298
  26.7 1.5 %shard_map.78 = (s32[32,64]{1,0:T(8,128)S(1)}, f32[64,32]{1,0:T(8,128)S(1)}, s32[32,64]{1,0:T(8,128)}, f32[8,1024]{1,0:T(8,128)S(1)}) custom-call(s32[1]{0:T(128)} %bitcast.where_ref, s32[4,8,128]{2,1,0:T(8,128)S(1)} %all_gather.3.codes_ref), custom_call_target="tpu_custom_call" | custom-call | tf_op jit(solution)/shard_map/pallas_call | solution.py:299
  28.9 3.6 %collective-permute-start.5 = (bf16[2,1,128,256]{3,2,1,0:T(8,128)(2,1)}, bf16[2,1,128,256]{3,2,1,0:T(8,128)(2,1)S(1)}, u32[]{:S(2)}, u32[]{:S(2)}) collective-permute-start(bf16[2,1,128,256]{3,2,1,0:T(8,128)(2,1)} %collective-permute-done.2.b2), channel_id=1, source_target_pairs={{0,1},{1,2},{2,3},{4,5},{5,6},{6,7},{8,9},{9,10},{10,11},{12,13},{... | collective-permute-start | bytes 393224 | tf_op jit(solution)/shard_map/ppermute | solution.py:23
  32.6 11.8 %shard_map.79 = (bf16[512,256]{1,0:T(8,128)(2,1)S(1)}, bf16[512,256]{1,0:T(8,128)(2,1)S(1)}, bf16[512,256]{1,0:T(8,128)(2,1)S(1)}, bf16[512,256]{1,0:T(8,128)(2,1)S(1)}) custom-call(s32[32,64]{1,0:T(8,128)S(1)} %get-tuple-element.23.ask_ref, bf16[4096,16,256]{2,1,0:T(8,128)(2,1)} %bitcast.15, f32[64,32]{1,0:T(8,128)S(1)} %get-tuple-element.24.low_ref), custom_call_target="tpu_custom_call" | custom-call | tf_op jit(solution)/shard_map/pallas_call | solution.py:311
  45.1 2.4 %collective-permute-start.6 = (bf16[2,1,128,256]{3,2,1,0:T(8,128)(2,1)}, bf16[2,1,128,256]{3,2,1,0:T(8,128)(2,1)S(1)}, u32[]{:S(2)}, u32[]{:S(2)}) collective-permute-start(bf16[2,1,128,256]{3,2,1,0:T(8,128)(2,1)} %collective-permute-done.b0), channel_id=1, source_target_pairs={{1,0},{2,1},{3,2},{5,4},{6,5},{7,6},{9,8},{10,9},{11,10},{13,12},{... | collective-permute-start | bytes 393224 | tf_op jit(solution)/shard_map/ppermute | solution.py:23
  47.6 1.9 %collective-permute-start.16 = (bf16[512,256]{1,0:T(8,128)(2,1)S(1)}, bf16[512,256]{1,0:T(8,128)(2,1)S(1)}, u32[]{:S(2)}, u32[]{:S(2)}) collective-permute-start(bf16[512,256]{1,0:T(8,128)(2,1)S(1)} %get-tuple-element.28), channel_id=1, source_target_pairs={{0,3},{1,0},{2,1},{3,2},{4,7},{5,4},{6,5},{7,6},{8,11},{9,8},{10,9... | collective-permute-start | bytes 786440 | tf_op jit(solution)/shard_map/ppermute | solution.py:28
  49.5 3.7 %collective-permute-done.6.c1 = bf16[2,1,128,256]{3,2,1,0:T(8,128)(2,1)S(1)} collective-permute-done((bf16[2,1,128,256]{3,2,1,0:T(8,128)(2,1)}, bf16[2,1,128,256]{3,2,1,0:T(8,128)(2,1)S(1)}, u32[]{:S(2)}, u32[]{:S(2)}) %collective-permute-start.6) | collective-permute-done | bytes 131104 | tf_op jit(solution)/shard_map/ppermute | solution.py:23
  53.2 6.1 %shard_map.77 = (bf16[2,4,128,256]{3,2,1,0:T(8,128)(2,1)S(1)}, bf16[2,1,128,256]{3,2,1,0:T(8,128)(2,1)}, bf16[2,2,128,256]{3,2,1,0:T(8,128)(2,1)}, bf16[2,1,128,256]{3,2,1,0:T(8,128)(2,1)}) custom-call(bf16[2,4,128,256]{3,2,1,0:T(8,128)(2,1)S(1)} %copy-done.2, bf16[2,1,128,256]{3,2,1,0:T(8,128)(2,1)} %collective-permute-done.b0, ...), custom_call_target="tpu_custom_call" | custom-call | tf_op jit(solution)/shard_map/pallas_call | solution.py:325
  60.0 3.1 %collective-permute-start.7 = (bf16[2,1,128,256]{3,2,1,0:T(8,128)(2,1)}, bf16[2,1,128,256]{3,2,1,0:T(8,128)(2,1)}, u32[]{:S(2)}, u32[]{:S(2)}) collective-permute-start(bf16[2,1,128,256]{3,2,1,0:T(8,128)(2,1)} %get-tuple-element.19.o0), channel_id=1, source_target_pairs={{0,4},{4,8},{8,12},{12,16},{16,20},{20,24},{24,28},{1,5},{5,9},{9,... | collective-permute-start | bytes 393224 | tf_op jit(solution)/shard_map/ppermute | solution.py:23
  63.1 4.6 %collective-permute-start.9 = (bf16[2,1,128,256]{3,2,1,0:T(8,128)(2,1)}, bf16[2,1,128,256]{3,2,1,0:T(8,128)(2,1)}, u32[]{:S(2)}, u32[]{:S(2)}) collective-permute-start(bf16[2,1,128,256]{3,2,1,0:T(8,128)(2,1)} %get-tuple-element.21.o2), channel_id=1, source_target_pairs={{0,4},{4,8},{8,12},{12,16},{16,20},{20,24},{24,28},{1,5},{5,9},{9,... | collective-permute-start | bytes 393224 | tf_op jit(solution)/shard_map/ppermute | solution.py:23
  68.5 2.0 %collective-permute-start.8 = (bf16[2,2,128,256]{3,2,1,0:T(8,128)(2,1)}, bf16[2,2,128,256]{3,2,1,0:T(8,128)(2,1)}, u32[]{:S(2)}, u32[]{:S(2)}) collective-permute-start(bf16[2,2,128,256]{3,2,1,0:T(8,128)(2,1)} %get-tuple-element.20.o1), channel_id=1, source_target_pairs={{0,4},{4,8},{8,12},{12,16},{16,20},{20,24},{24,28},{1,5},{5,9},{9,... | collective-permute-start | bytes 786440 | tf_op jit(solution)/shard_map/ppermute | solution.py:23
  71.2 1.9 %collective-permute-start.11 = (bf16[2,1,128,256]{3,2,1,0:T(8,128)(2,1)}, bf16[2,1,128,256]{3,2,1,0:T(8,128)(2,1)}, u32[]{:S(2)}, u32[]{:S(2)}) collective-permute-start(bf16[2,1,128,256]{3,2,1,0:T(8,128)(2,1)} %get-tuple-element.19.o0), channel_id=1, source_target_pairs={{1,0},{2,1},{3,2},{5,4},{6,5},{7,6},{9,8},{10,9},{11,10},{13,12},{... | collective-permute-start | bytes 393224 | tf_op jit(solution)/shard_map/ppermute | solution.py:23
  73.9 3.6 %collective-permute-start.10 = (bf16[2,1,128,256]{3,2,1,0:T(8,128)(2,1)}, bf16[2,1,128,256]{3,2,1,0:T(8,128)(2,1)}, u32[]{:S(2)}, u32[]{:S(2)}) collective-permute-start(bf16[2,1,128,256]{3,2,1,0:T(8,128)(2,1)} %get-tuple-element.21.o2), channel_id=1, source_target_pairs={{0,1},{1,2},{2,3},{4,5},{5,6},{6,7},{8,9},{9,10},{10,11},{12,13},{... | collective-permute-start | bytes 393224 | tf_op jit(solution)/shard_map/ppermute | solution.py:23
  77.5 1.9 %collective-permute-start.13 = (bf16[2,1,128,256]{3,2,1,0:T(8,128)(2,1)}, bf16[2,1,128,256]{3,2,1,0:T(8,128)(2,1)}, u32[]{:S(2)}, u32[]{:S(2)}) collective-permute-start(bf16[2,1,128,256]{3,2,1,0:T(8,128)(2,1)} %collective-permute-done.7.b0), channel_id=1, source_target_pairs={{1,0},{2,1},{3,2},{5,4},{6,5},{7,6},{9,8},{10,9},{11,10},{13,12},{... | collective-permute-start | bytes 393224 | tf_op jit(solution)/shard_map/ppermute | solution.py:23
  79.5 3.6 %collective-permute-start.12 = (bf16[2,1,128,256]{3,2,1,0:T(8,128)(2,1)}, bf16[2,1,128,256]{3,2,1,0:T(8,128)(2,1)}, u32[]{:S(2)}, u32[]{:S(2)}) collective-permute-start(bf16[2,1,128,256]{3,2,1,0:T(8,128)(2,1)} %collective-permute-done.9.b2), channel_id=1, source_target_pairs={{0,1},{1,2},{2,3},{4,5},{5,6},{6,7},{8,9},{9,10},{10,11},{12,13},{... | collective-permute-start | bytes 393224 | tf_op jit(solution)/shard_map/ppermute | solution.py:23
  83.1 2.5 %all-to-all-start = ((s32[32,1,64]{2,1,0:T(1,128)}), s32[32,1,64]{2,1,0:T(1,128)S(1)}, u32[]{:S(2)}, u32[]{:S(2)}) async-start(s32[32,1,64]{2,1,0:T(1,128)} %bitcast.7), calls=%async_computation | async-start | bytes 32768 | tf_op jit(solution)/shard_map/all_to_all | solution.py:323
  90.1 2.5 %shard_map.80 = (bf16[1024,256]{1,0:T(8,128)(2,1)S(1)}, bf16[2048,256]{1,0:T(8,128)(2,1)S(1)}) custom-call(f32[8,1024]{1,0:T(8,128)S(1)} %copy-done.20, bf16[512,256]{1,0:T(8,128)(2,1)S(1)} %copy-done.12, bf16[512,256]{1,0:T(8,128)(2,1)S(1)} %copy-done.14, bf16[512,256]{1,0:T(8,128)(2,1)S(1)} %copy-done.16, bf16[512,256]{1,0:T(8,128)(2,1)S(1)} %copy-done.18), custom_call_target="tpu_custom_call" | custom-call | tf_op jit(solution)/shard_map/pallas_call | solution.py:335
  95.3 6.3 %shard_map.81 = (bf16[2,4,128,256]{3,2,1,0:T(8,128)(2,1)S(1)}, bf16[2048,256]{1,0:T(8,128)(2,1)S(1)}) custom-call(bf16[2,4,128,256]{3,2,1,0:T(8,128)(2,1)S(1)} %copy-done.5, bf16[2,1,128,256]{3,2,1,0:T(8,128)(2,1)} %get-tuple-element.19.o0, bf16[2,2,128,256]{3,2,1,0:T(8,128)(2,1)} %get-tuple-element.20.o1, bf16[2,1,128,256]{3,2,1,0:T(8,128)(2,1)} %get-tuple-element.21.o2, ...), custom_call_target="tpu_custom_call" | custom-call | tf_op jit(solution)/shard_map/pallas_call | solution.py:346
  103.4 5.2 %all-to-all-start.1 = ((bf16[32,64,256]{2,1,0:T(8,128)(2,1)}), bf16[32,64,256]{2,1,0:T(8,128)(2,1)S(1)}, u32[]{:S(2)}, u32[]{:S(2)}) async-start(bf16[32,64,256]{2,1,0:T(8,128)(2,1)} %bitcast.12), calls=%async_computation.1 | async-start | bytes 2097152 | tf_op jit(solution)/shard_map/all_to_all | solution.py:354
  110.1 1.0 copy-done.6
  111.1 1.0 copy-done.8
  112.2 1.0 copy-done.10
  113.2 3.1 %shard_map.82 = bf16[1024,256]{1,0:T(8,128)(2,1)} custom-call(bf16[1024,256]{1,0:T(8,128)(2,1)S(1)} %bitcast.14, bf16[1024,256]{1,0:T(8,128)(2,1)S(1)} %copy-done.8, bf16[1024,256]{1,0:T(8,128)(2,1)S(1)} %bitcast.13), custom_call_target="tpu_custom_call" | custom-call | tf_op jit(solution)/shard_map/pallas_call | solution.py:357
  116.3 17.7 %all-to-all-done.1 = bf16[32,64,256]{2,1,0:T(8,128)(2,1)S(1)} async-done(((bf16[32,64,256]{2,1,0:T(8,128)(2,1)}), bf16[32,64,256]{2,1,0:T(8,128)(2,1)S(1)}, u32[]{:S(2)}, u32[]{:S(2)}) %all-to-all-start.1) | async-done | bytes 1048608 | tf_op jit(solution)/shard_map/all_to_all | solution.py:354
  134.0 18.0 %shard_map.83 = bf16[8192,256]{1,0:T(8,128)(2,1)} custom-call(s32[1,2048]{1,0:T(1,128)S(1)} %reshape.36.target, bf16[2048,256]{1,0:T(8,128)(2,1)S(1)} %bitcast.11), custom_call_target="tpu_custom_call" | custom-call | tf_op jit(solution)/shard_map/pallas_call | solution.py:365
  (63 shorter events, 14.7 us)
Async XLA Ops:
  2.3 26.6 %collective-permute-start.2 = (bf16[2,1,128,256]{3,2,1,0:T(8,128)(2,1)}, bf16[2,1,128,256]{3,2,1,0:T(8,128)(2,1)}, u32[]{:S(2)}, u32[]{:S(2)}) collective-permute-start(bf16[2,1,128,256]{3,2,1,0:T(8,128)(2,1)} %get-tuple-element.34), channel_id=1, source_target_pairs={{0,4},{4,8},{8,12},{12,16},{16,20},{20,24},{24,28},{1,5},{5,9},{9,... | collective-permute-start | bytes 393224 | tf_op jit(solution)/shard_map/ppermute | solution.py:23
  6.9 38.1 %collective-permute-start.3 = (bf16[2,1,128,256]{3,2,1,0:T(8,128)(2,1)}, bf16[2,1,128,256]{3,2,1,0:T(8,128)(2,1)}, u32[]{:S(2)}, u32[]{:S(2)}) collective-permute-start(bf16[2,1,128,256]{3,2,1,0:T(8,128)(2,1)} %get-tuple-element.34), channel_id=1, source_target_pairs={{0,1},{1,2},{2,3},{4,5},{5,6},{6,7},{8,9},{9,10},{10,11},{12,13},{... | collective-permute-start | bytes 393224 | tf_op jit(solution)/shard_map/ppermute | solution.py:23
  10.9 36.6 %collective-permute-start.4 = (bf16[2,1,128,256]{3,2,1,0:T(8,128)(2,1)}, bf16[2,1,128,256]{3,2,1,0:T(8,128)(2,1)}, u32[]{:S(2)}, u32[]{:S(2)}) collective-permute-start(bf16[2,1,128,256]{3,2,1,0:T(8,128)(2,1)} %get-tuple-element.35), channel_id=1, source_target_pairs={{1,0},{2,1},{3,2},{5,4},{6,5},{7,6},{9,8},{10,9},{11,10},{13,12},{... | collective-permute-start | bytes 393224 | tf_op jit(solution)/shard_map/ppermute | solution.py:23
  12.8 32.2 %collective-permute-start = (bf16[2,1,128,256]{3,2,1,0:T(8,128)(2,1)}, bf16[2,1,128,256]{3,2,1,0:T(8,128)(2,1)}, u32[]{:S(2)}, u32[]{:S(2)}) collective-permute-start(bf16[2,1,128,256]{3,2,1,0:T(8,128)(2,1)} %get-tuple-element.35), channel_id=1, source_target_pairs={{0,4},{4,8},{8,12},{12,16},{16,20},{20,24},{24,28},{1,5},{5,9},{9,... | collective-permute-start | bytes 393224 | tf_op jit(solution)/shard_map/ppermute | solution.py:23
  17.7 35.5 %collective-permute-start.1 = (bf16[2,2,128,256]{3,2,1,0:T(8,128)(2,1)}, bf16[2,2,128,256]{3,2,1,0:T(8,128)(2,1)}, u32[]{:S(2)}, u32[]{:S(2)}) collective-permute-start(bf16[2,2,128,256]{3,2,1,0:T(8,128)(2,1)} %slice.10), channel_id=1, source_target_pairs={{0,4},{4,8},{8,12},{12,16},{16,20},{20,24},{24,28},{1,5},{5,9},{9,... | collective-permute-start | bytes 786440 | tf_op jit(solution)/shard_map/ppermute | solution.py:23
  28.9 18.7 %collective-permute-start.5 = (bf16[2,1,128,256]{3,2,1,0:T(8,128)(2,1)}, bf16[2,1,128,256]{3,2,1,0:T(8,128)(2,1)S(1)}, u32[]{:S(2)}, u32[]{:S(2)}) collective-permute-start(bf16[2,1,128,256]{3,2,1,0:T(8,128)(2,1)} %collective-permute-done.2.b2), channel_id=1, source_target_pairs={{0,1},{1,2},{2,3},{4,5},{5,6},{6,7},{8,9},{9,10},{10,11},{12,13},{... | collective-permute-start | bytes 393224 | tf_op jit(solution)/shard_map/ppermute | solution.py:23
  32.5 20.6 %copy-start = (bf16[3,3,3,256,256]{4,3,2,1,0:T(8,128)(2,1)S(1)}, bf16[3,3,3,256,256]{4,3,2,1,0:T(8,128)(2,1)}, u32[]{:S(2)}) copy-start(bf16[3,3,3,256,256]{4,3,2,1,0:T(8,128)(2,1)} %weight.2) | copy-start | bytes 10616836
  32.6 20.6 %copy-start.2 = (bf16[2,4,128,256]{3,2,1,0:T(8,128)(2,1)S(1)}, bf16[2,4,128,256]{3,2,1,0:T(8,128)(2,1)}, u32[]{:S(2)}) copy-start(bf16[2,4,128,256]{3,2,1,0:T(8,128)(2,1)} %video.1) | copy-start | bytes 1572868
  45.0 48.5 %copy-start.1 = (bf16[3,3,3,256,256]{4,3,2,1,0:T(8,128)(2,1)S(1)}, bf16[3,3,3,256,256]{4,3,2,1,0:T(8,128)(2,1)}, u32[]{:S(2)}) copy-start(bf16[3,3,3,256,256]{4,3,2,1,0:T(8,128)(2,1)} %weight.3) | copy-start | bytes 10616836
  45.0 22.7 %collective-permute-start.14 = (bf16[512,256]{1,0:T(8,128)(2,1)S(1)}, bf16[512,256]{1,0:T(8,128)(2,1)S(1)}, u32[]{:S(2)}, u32[]{:S(2)}) collective-permute-start(bf16[512,256]{1,0:T(8,128)(2,1)S(1)} %get-tuple-element.26), channel_id=1, source_target_pairs={{0,1},{1,2},{2,3},{3,0},{4,5},{5,6},{6,7},{7,4},{8,9},{9,10},{10,1... | collective-permute-start | bytes 786440 | tf_op jit(solution)/shard_map/ppermute | solution.py:28
  45.1 8.1 %collective-permute-start.6 = (bf16[2,1,128,256]{3,2,1,0:T(8,128)(2,1)}, bf16[2,1,128,256]{3,2,1,0:T(8,128)(2,1)S(1)}, u32[]{:S(2)}, u32[]{:S(2)}) collective-permute-start(bf16[2,1,128,256]{3,2,1,0:T(8,128)(2,1)} %collective-permute-done.b0), channel_id=1, source_target_pairs={{1,0},{2,1},{3,2},{5,4},{6,5},{7,6},{9,8},{10,9},{11,10},{13,12},{... | collective-permute-start | bytes 393224 | tf_op jit(solution)/shard_map/ppermute | solution.py:23
  47.5 23.0 %collective-permute-start.15 = (bf16[512,256]{1,0:T(8,128)(2,1)S(1)}, bf16[512,256]{1,0:T(8,128)(2,1)S(1)}, u32[]{:S(2)}, u32[]{:S(2)}) collective-permute-start(bf16[512,256]{1,0:T(8,128)(2,1)S(1)} %get-tuple-element.27), channel_id=1, source_target_pairs={{0,2},{1,3},{2,0},{3,1},{4,6},{5,7},{6,4},{7,5},{8,10},{9,11},{10,... | collective-permute-start | bytes 786440 | tf_op jit(solution)/shard_map/ppermute | solution.py:28
  47.6 25.6 %collective-permute-start.16 = (bf16[512,256]{1,0:T(8,128)(2,1)S(1)}, bf16[512,256]{1,0:T(8,128)(2,1)S(1)}, u32[]{:S(2)}, u32[]{:S(2)}) collective-permute-start(bf16[512,256]{1,0:T(8,128)(2,1)S(1)} %get-tuple-element.28), channel_id=1, source_target_pairs={{0,3},{1,0},{2,1},{3,2},{4,7},{5,4},{6,5},{7,6},{8,11},{9,8},{10,9... | collective-permute-start | bytes 786440 | tf_op jit(solution)/shard_map/ppermute | solution.py:28
  60.0 17.5 %collective-permute-start.7 = (bf16[2,1,128,256]{3,2,1,0:T(8,128)(2,1)}, bf16[2,1,128,256]{3,2,1,0:T(8,128)(2,1)}, u32[]{:S(2)}, u32[]{:S(2)}) collective-permute-start(bf16[2,1,128,256]{3,2,1,0:T(8,128)(2,1)} %get-tuple-element.19.o0), channel_id=1, source_target_pairs={{0,4},{4,8},{8,12},{12,16},{16,20},{20,24},{24,28},{1,5},{5,9},{9,... | collective-permute-start | bytes 393224 | tf_op jit(solution)/shard_map/ppermute | solution.py:23
  63.1 16.3 %collective-permute-start.9 = (bf16[2,1,128,256]{3,2,1,0:T(8,128)(2,1)}, bf16[2,1,128,256]{3,2,1,0:T(8,128)(2,1)}, u32[]{:S(2)}, u32[]{:S(2)}) collective-permute-start(bf16[2,1,128,256]{3,2,1,0:T(8,128)(2,1)} %get-tuple-element.21.o2), channel_id=1, source_target_pairs={{0,4},{4,8},{8,12},{12,16},{16,20},{20,24},{24,28},{1,5},{5,9},{9,... | collective-permute-start | bytes 393224 | tf_op jit(solution)/shard_map/ppermute | solution.py:23
  68.5 25.0 %collective-permute-start.8 = (bf16[2,2,128,256]{3,2,1,0:T(8,128)(2,1)}, bf16[2,2,128,256]{3,2,1,0:T(8,128)(2,1)}, u32[]{:S(2)}, u32[]{:S(2)}) collective-permute-start(bf16[2,2,128,256]{3,2,1,0:T(8,128)(2,1)} %get-tuple-element.20.o1), channel_id=1, source_target_pairs={{0,4},{4,8},{8,12},{12,16},{16,20},{20,24},{24,28},{1,5},{5,9},{9,... | collective-permute-start | bytes 786440 | tf_op jit(solution)/shard_map/ppermute | solution.py:23
  71.2 22.3 %collective-permute-start.11 = (bf16[2,1,128,256]{3,2,1,0:T(8,128)(2,1)}, bf16[2,1,128,256]{3,2,1,0:T(8,128)(2,1)}, u32[]{:S(2)}, u32[]{:S(2)}) collective-permute-start(bf16[2,1,128,256]{3,2,1,0:T(8,128)(2,1)} %get-tuple-element.19.o0), channel_id=1, source_target_pairs={{1,0},{2,1},{3,2},{5,4},{6,5},{7,6},{9,8},{10,9},{11,10},{13,12},{... | collective-permute-start | bytes 393224 | tf_op jit(solution)/shard_map/ppermute | solution.py:23
  73.9 19.6 %collective-permute-start.10 = (bf16[2,1,128,256]{3,2,1,0:T(8,128)(2,1)}, bf16[2,1,128,256]{3,2,1,0:T(8,128)(2,1)}, u32[]{:S(2)}, u32[]{:S(2)}) collective-permute-start(bf16[2,1,128,256]{3,2,1,0:T(8,128)(2,1)} %get-tuple-element.21.o2), channel_id=1, source_target_pairs={{0,1},{1,2},{2,3},{4,5},{5,6},{6,7},{8,9},{9,10},{10,11},{12,13},{... | collective-permute-start | bytes 393224 | tf_op jit(solution)/shard_map/ppermute | solution.py:23
  77.5 16.0 %collective-permute-start.13 = (bf16[2,1,128,256]{3,2,1,0:T(8,128)(2,1)}, bf16[2,1,128,256]{3,2,1,0:T(8,128)(2,1)}, u32[]{:S(2)}, u32[]{:S(2)}) collective-permute-start(bf16[2,1,128,256]{3,2,1,0:T(8,128)(2,1)} %collective-permute-done.7.b0), channel_id=1, source_target_pairs={{1,0},{2,1},{3,2},{5,4},{6,5},{7,6},{9,8},{10,9},{11,10},{13,12},{... | collective-permute-start | bytes 393224 | tf_op jit(solution)/shard_map/ppermute | solution.py:23
  79.5 14.0 %collective-permute-start.12 = (bf16[2,1,128,256]{3,2,1,0:T(8,128)(2,1)}, bf16[2,1,128,256]{3,2,1,0:T(8,128)(2,1)}, u32[]{:S(2)}, u32[]{:S(2)}) collective-permute-start(bf16[2,1,128,256]{3,2,1,0:T(8,128)(2,1)} %collective-permute-done.9.b2), channel_id=1, source_target_pairs={{0,1},{1,2},{2,3},{4,5},{5,6},{6,7},{8,9},{9,10},{10,11},{12,13},{... | collective-permute-start | bytes 393224 | tf_op jit(solution)/shard_map/ppermute | solution.py:23
  83.1 20.3 %all-to-all-start = ((s32[32,1,64]{2,1,0:T(1,128)}), s32[32,1,64]{2,1,0:T(1,128)S(1)}, u32[]{:S(2)}, u32[]{:S(2)}) async-start(s32[32,1,64]{2,1,0:T(1,128)} %bitcast.7), calls=%async_computation | async-start | bytes 32768 | tf_op jit(solution)/shard_map/all_to_all | solution.py:323
  85.6 1.0 copy-start.12
  86.5 0.9 copy-start.14
  87.5 0.9 copy-start.16
  88.4 0.9 copy-start.18
  92.7 0.8 copy-start.7
  93.5 1.0 copy-start.5
  101.7 1.0 copy-start.3
  103.4 30.6 %all-to-all-start.1 = ((bf16[32,64,256]{2,1,0:T(8,128)(2,1)}), bf16[32,64,256]{2,1,0:T(8,128)(2,1)S(1)}, u32[]{:S(2)}, u32[]{:S(2)}) async-start(bf16[32,64,256]{2,1,0:T(8,128)(2,1)} %bitcast.12), calls=%async_computation.1 | async-start | bytes 2097152 | tf_op jit(solution)/shard_map/all_to_all | solution.py:354
  110.1 1.0 copy-start.6
  111.1 1.0 copy-start.8
  112.2 1.0 copy-start.10
  (9 other events, 6.6 us)
